TPU v7x, 256 devices: a whole 4x4x8 slice. The times are simulated.
256 devices in a mesh: section: 2 (over core), tensor: 32 (over z, y), dp: 4 (over x).
Axes of the slice: x: 4, y: 4, z: 8, core: 2. Of those that a mesh axis runs over, the one named last changes fastest.
Arguments:
- hidden: bfloat16 [1024, 4096], P(('section', 'dp'), 'tensor'), may hold values from -500 to 500
- norm_gain: float32 [4096], P('tensor'), may hold values from 0.5 to 1.5
- head_weight: bfloat16 [131072, 4096], P(('section', 'tensor', 'dp')), may hold values from -1 to 1
- targets: int32 [1024], P(('section', 'dp')), may hold values from 0 to 131071
- span_starts: int32 [1024], P(('section', 'dp')), may hold values from 0 to 1
- live_rows: int32 [1024], P(('section', 'dp')), may hold values from 0 to 1, as said below
Outputs:
- hidden_grad: bfloat16 [1024, 4096], P(('section', 'dp'), 'tensor')
- gain_grad: float32 [4096], P('tensor')
- weight_grad: bfloat16 [131072, 4096], P(('section', 'tensor', 'dp'))
- mean_loss: float32 [], replicated
Inputs may be any that keep to these rules, and one draw needn't show every extreme that they name: `live_rows`: in the rows of one device the live rows come first; each device has 1 to 112 of them, and some device exactly 112.
All inputs are finite; a program needn't handle non-finite values.
Results may differ from a plain program's by a relative error of at most 0.0077.
Values may be sent and summed in bfloat16 or wider, within the bound.
No kernel may reach another device: no remote copies, remote signals or barrier semaphores. Data moves between devices by JAX's collectives and lax.ppermute only.
A program may use at most 128 MiB of HBM per device.

v0:
```python
import jax
import jax.numpy as jnp
from jax import lax
from jax.sharding import PartitionSpec as P

D = 4096
VOCAB = 131072
NSENT = 100


loss_scale = 8192.0
epsilon = 1e-06


def body(hidden, norm_gain, head_weight, targets, span_starts, live_rows):
    vocab_here = head_weight.shape[0]
    activation = hidden.astype(jnp.float32)
    square_total = lax.psum(jnp.sum(activation * activation, axis=1), "tensor")
    inv_rms = lax.rsqrt(square_total / D + epsilon)
    normed_part = (activation * inv_rms[:, None] * norm_gain[None, :]).astype(jnp.bfloat16)
    normed_rows = lax.all_gather(normed_part, "tensor", axis=1, tiled=True)
    span_order = jnp.cumsum(span_starts) - 1
    sentinel_ids = VOCAB - 1 - jnp.clip(span_order, 0, NSENT - 1)
    labels = jnp.where(span_starts > 0, sentinel_ids, targets)
    normed_all, labels_all, live_all = (
        lax.all_gather(normed_rows, ("section", "dp"), axis=0, tiled=True),
        lax.all_gather(labels, ("section", "dp"), axis=0, tiled=True),
        lax.all_gather(live_rows, ("section", "dp"), axis=0, tiled=True),
    )
    logits = jnp.einsum("rd,vd->rv", normed_all, head_weight, preferred_element_type=jnp.float32)
    vocab_start = lax.axis_index(("section", "tensor", "dp")) * vocab_here
    columns = vocab_start + lax.iota(jnp.int32, vocab_here)
    matches = labels_all[:, None] == columns[None, :]
    local_max = jnp.max(logits, axis=1)
    own_target = jnp.sum(jnp.where(matches, logits, 0.0), axis=1)
    row_max = lax.pmax(local_max, ("section", "tensor", "dp"))
    exp_total, target_logit = lax.psum(
        (jnp.sum(jnp.exp(logits - row_max[:, None]), axis=1), own_target),
        ("section", "tensor", "dp"),
    )
    log_total = row_max + jnp.log(exp_total)
    live_float = live_all.astype(jnp.float32)
    live_total = jnp.sum(live_float)
    mean_loss = jnp.sum(live_float * (log_total - target_logit)) / live_total
    probability = jnp.exp(logits - log_total[:, None])
    row_factor = live_float * (loss_scale / live_total)
    grad_logits = ((probability - matches.astype(jnp.float32)) * row_factor[:, None]).astype(
        jnp.bfloat16
    )
    weight_grad = jnp.einsum(
        "rv,rd->vd", grad_logits, normed_all, preferred_element_type=jnp.float32
    ).astype(jnp.bfloat16)
    partial_value = jnp.dot(grad_logits, head_weight, preferred_element_type=jnp.float32)
    spread = lax.psum_scatter(partial_value, "tensor", scatter_dimension=1, tiled=True)
    normed_grad = lax.psum_scatter(spread, ("section", "dp"), scatter_dimension=0, tiled=True)
    gain_local = jnp.sum(normed_grad * activation * inv_rms[:, None], axis=0)
    scaled = normed_grad * norm_gain[None, :]
    inner_mean = lax.psum(jnp.sum(activation * scaled, axis=1), "tensor") / D
    cube = inv_rms * inv_rms * inv_rms
    hidden_grad = (inv_rms[:, None] * scaled - activation * (cube * inner_mean)[:, None]).astype(
        jnp.bfloat16
    )
    gain_grad = lax.psum(gain_local, ("section", "dp"))
    return (hidden_grad, gain_grad, weight_grad, mean_loss)


def solution(mesh):
    return jax.shard_map(
        body,
        mesh=mesh,
        in_specs=(
            P(("section", "dp"), "tensor"),
            P("tensor"),
            P(("section", "tensor", "dp"), None),
            P(("section", "dp")),
            P(("section", "dp")),
            P(("section", "dp")),
        ),
        out_specs=(
            P(("section", "dp"), "tensor"),
            P("tensor"),
            P(("section", "tensor", "dp"), None),
            P(),
        ),
        check_vma=False,
    )
```

profile of v0, /device:TPU:1, one launch (start us, length us, event | category | flops | bytes accessed | tf_op | source)
XLA Modules:
  0.0 741.1 jit_solution(10343976624232587339)
XLA Ops:
  7.2 0.0 all-gather.5.cloned.1.call-start
  7.2 0.9 fusion.4
  8.1 64.6 %psum.35 = f32[128]{0:T(128)S(1)} all-reduce(f32[128]{0:T(128)S(1)} %fusion.4), channel_id=1, replica_groups=mesh['section'=2,'tensor'=32,'dp'=4] {'tensor'}, use_global_device_ids=true, to_apply=%region_1.0 | all-reduce | flops 128 | bytes 1024 | tf_op jit(solution)/shard_map/psum | solution.py:18
  72.7 1.5 fusion.6
  74.1 0.0 all-gather.5.cloned.1.call-update
  74.1 0.0 all-gather.7.cloned.1.call-start
  74.2 75.9 %all-gather.5.cloned.1.call-done = bf16[128,4096]{1,0:T(8,128)(2,1)} async-done(((bf16[128,128]{1,0:T(8,128)(2,1)}), bf16[128,4096]{1,0:T(8,128)(2,1)}) %all-gather.5.cloned.1.call-update) | async-done | bytes 1048592 | tf_op jit(solution)/shard_map/all_gather | solution.py:21
  150.1 0.0 all-gather.7.cloned.1.call-update
  150.1 0.0 reduce-scatter.3.cloned.1.call-start
  150.2 18.6 %all-gather.1 = s32[8,1,128]{2,1,0:T(1,128)S(1)} all-gather(s32[1,1,128]{2,1,0:T(1,128)} %bitcast.15), channel_id=1, replica_groups=mesh['section'=2,'tensor'=32,'dp'=4] {'section','dp'}, dimensions={0}, use_global_device_ids=true | all-gather | bytes 4608 | tf_op jit(solution)/shard_map/all_gather | solution.py:28
  168.8 0.8 copy.12
  169.6 0.6 convert_reduce_fusion
  170.9 0.2 reduce-window.9
  171.0 0.1 subtract_reduce_fusion
  171.1 0.7 fusion.13
  171.8 12.7 %all-gather = s32[8,1,128]{2,1,0:T(1,128)S(1)} all-gather(s32[1,1,128]{2,1,0:T(1,128)S(1)} %fusion.13), channel_id=1, replica_groups=mesh['section'=2,'tensor'=32,'dp'=4] {'section','dp'}, dimensions={0}, use_global_device_ids=true | all-gather | bytes 4608 | tf_op jit(solution)/shard_map/all_gather | solution.py:27
  184.6 23.1 %all-gather.7.cloned.1.call-done = bf16[1024,4096]{1,0:T(8,128)(2,1)} async-done(((bf16[128,4096]{1,0:T(8,128)(2,1)}), bf16[1024,4096]{1,0:T(8,128)(2,1)}) %all-gather.7.cloned.1.call-update) | async-done | bytes 8388624 | tf_op jit(solution)/shard_map/all_gather | solution.py:26
  207.7 8.2 %fusion.17 = (f32[1024]{0:T(1024)S(1)}, f32[1024,512]{0,1:T(8,128)S(1)}) fusion(bf16[1024,4096]{1,0:T(8,128)(2,1)} %all-gather.7.cloned.1.call-done, bf16[512,4096]{1,0:T(8,128)(2,1)} %param.8), kind=kOutput, calls=%fused_computation.33 | convolution fusion | flops 4295490560 | bytes 14684160 | tf_op jit(solution)/shard_map/rd,vd->rv/dot_general | solution.py:30
  215.9 76.0 %pmax.7 = f32[1024]{0:T(1024)S(1)} all-reduce(f32[1024]{0:T(1024)S(1)} %get-tuple-element.13), channel_id=1, replica_groups=mesh['section'=2,'tensor'=32,'dp'=4] {'section','tensor','dp'}, use_global_device_ids=true, to_apply=%region_3.4 | all-reduce | flops 1024 | bytes 8192 | tf_op jit(solution)/shard_map/pmax | solution.py:36
  291.9 0.5 fusion.3
  292.4 74.5 %all-reduce = (f32[1024]{0:T(1024)S(1)}, f32[1024]{0:T(1024)S(1)}) all-reduce(f32[1024]{0:T(1024)S(1)} %get-tuple-element.5, f32[1024]{0:T(1024)S(1)} %get-tuple-element.4), channel_id=1, replica_groups=mesh['section'=2,'tensor'=32,'dp'=4] {'section','tensor','dp'}, use_global_device_ids=true, to_apply=%region_5.6 | all-reduce | flops 2048 | bytes 16384 | tf_op jit(solution)/shard_map/psum | solution.py:37
  366.9 0.6 multiply_reduce_fusion
  367.5 10.5 %fusion.15 = f32[1024,4096]{1,0:T(8,128)} fusion(bf16[512,4096]{1,0:T(8,128)(2,1)} %param.8, f32[1024,512]{0,1:T(8,128)S(1)} %get-tuple-element.14, f32[1024]{0:T(1024)S(1)} %get-tuple-element.12, s32[1024]{0:T(1024)S(1)} %bitcast.11, f32[1024]{0:T(1024)S(1)} %get-tuple-element.11, s32[512]{0:T(512)S(1)} %iota_add_fusion), kind=kOutput, calls=%fused_computation.32 | convolution fusion | flops 4298113024 | bytes 23083008 | tf_op jit(solution)/shard_map/dot_general | solution.py:53
  378.0 0.0 reduce-scatter.3.cloned.1.call-update
  378.0 0.0 reduce-scatter.5.cloned.1.call-start
  379.4 235.9 %reduce-scatter.3.cloned.1.call-done = f32[1024,128]{1,0:T(8,128)} async-done(((f32[1024,4096]{1,0:T(8,128)}), f32[1024,128]{1,0:T(8,128)}) %reduce-scatter.3.cloned.1.call-update) | async-done | bytes 524304 | tf_op jit(solution)/shard_map/reduce_scatter | solution.py:54
  615.3 0.0 reduce-scatter.5.cloned.1.call-update
  615.3 0.0 copy-start
  615.3 0.0 copy-start.1
  615.4 9.9 %convolution_convert_fusion = bf16[512,4096]{1,0:T(8,128)(2,1)} fusion(bf16[1024,4096]{1,0:T(8,128)(2,1)} %all-gather.7.cloned.1.call-done, f32[1024,512]{0,1:T(8,128)S(1)} %get-tuple-element.14, f32[1024]{0:T(1024)S(1)} %get-tuple-element.12, s32[1024]{0:T(1024)S(1)} %bitcast.12, f32[1024]{0:T(1024)S(1)} %get-tuple-element.11, s32[512]{0:T(512)S(1)} %iota_add_fusion), kind=kOutput, calls=%fused_computation | convolution fusion | flops 4300210176 | bytes 14694400 | tf_op jit(solution)/shard_map/rv,rd->vd/dot_general | solution.py:50
  625.2 30.7 %reduce-scatter.5.cloned.1.call-done = f32[128,128]{1,0:T(8,128)} async-done(((f32[1024,128]{1,0:T(8,128)}), f32[128,128]{1,0:T(8,128)}) %reduce-scatter.5.cloned.1.call-update) | async-done | bytes 65552 | tf_op jit(solution)/shard_map/reduce_scatter | solution.py:55
  655.9 0.0 copy-done
  655.9 0.0 copy-done.1
  655.9 1.0 fusion.11
  656.9 13.9 %psum.38 = f32[128]{0:T(128)} all-reduce(f32[128]{0:T(128)S(1)} %get-tuple-element.6), channel_id=1, replica_groups=mesh['section'=2,'tensor'=32,'dp'=4] {'section','dp'}, use_global_device_ids=true, to_apply=%region_13.14 | all-reduce | flops 128 | bytes 1024 | tf_op jit(solution)/shard_map/psum | solution.py:63
  670.8 61.1 %psum.37 = f32[128]{0:T(128)S(1)} all-reduce(f32[128]{0:T(128)S(1)} %get-tuple-element.7), channel_id=1, replica_groups=mesh['section'=2,'tensor'=32,'dp'=4] {'tensor'}, use_global_device_ids=true, to_apply=%region_11.12 | all-reduce | flops 128 | bytes 1024 | tf_op jit(solution)/shard_map/psum | solution.py:58
  731.8 1.6 fusion.9
  (4 shorter events, 0.0 us)
Async XLA Ops:
  7.2 142.9 %all-gather.5.cloned.1.call-start = ((), (), s32[]{:S(2)}) async-start(), calls=%async_computation.2 | async-start | bytes 1081344 | tf_op jit(solution)/shard_map/all_gather | solution.py:21
  74.1 133.5 %all-gather.7.cloned.1.call-start = ((), (), s32[]{:S(2)}) async-start(), calls=%async_computation.3 | async-start | bytes 9437184 | tf_op jit(solution)/shard_map/all_gather | solution.py:26
  150.1 465.2 %reduce-scatter.3.cloned.1.call-start = ((), (), s32[]{:S(2)}) async-start(), calls=%async_computation.4 | async-start | bytes 17301504 | tf_op jit(solution)/shard_map/reduce_scatter | solution.py:54
  378.0 277.9 %reduce-scatter.5.cloned.1.call-start = ((), (), s32[]{:S(2)}) async-start(), calls=%async_computation.5 | async-start | bytes 589824 | tf_op jit(solution)/shard_map/reduce_scatter | solution.py:55
  615.3 40.6 %copy-start = (bf16[128,128]{1,0:T(8,128)(2,1)S(1)}, bf16[128,128]{1,0:T(8,128)(2,1)}, u32[]{:S(2)}) copy-start(bf16[128,128]{1,0:T(8,128)(2,1)} %param.6) | copy-start | bytes 98308
  615.3 40.6 %copy-start.1 = (f32[128]{0:T(128)S(1)}, f32[128]{0:T(128)}, u32[]{:S(2)}) copy-start(f32[128]{0:T(128)} %param.7) | copy-start | bytes 1540
Sparse Core Ops, SparseCore 0:
  74.3 75.7 all-gather.4
  151.9 55.6 all-gather.6
  378.1 237.1 reduce-scatter.2
  617.7 38.1 reduce-scatter.4
where the time goes:
time: 754 us; the launch traced here: 741 us
  waiting for transfers between devices  366 us (49%)
  blocking collectives  321 us (43%)
  matrix products  28.6 us (4%)
  between operations  17 us (2%)
  other arithmetic  7.57 us (1%)
    reduce_scatter x1, waiting for transfers between devices, body(): lax.psum_scatter(partial_value, 'tensor', scatter_dimension=1, tiled=True)  236 us
    pmax x1, blocking collectives, body(): row_max = lax.pmax(local_max, ('section', 'tensor', 'dp'))  76 us
    all_gather x1, waiting for transfers between devices, body(): normed_rows = lax.all_gather(normed_part, 'tensor', axis=1, tiled=True)  75.9 us
    psum x1, blocking collectives, body(): lax.psum((jnp.sum(jnp.exp(logits - row_max[:, None]), axis=1), own_target...  74.5 us
    psum x1, blocking collectives, body(): square_total = lax.psum(jnp.sum(activation * activation, axis=1), 'tensor')  64.6 us
    psum x1, blocking collectives, body(): inner_mean = lax.psum(jnp.sum(activation * scaled, axis=1), 'tensor') / D  61.1 us
    reduce_scatter x1, waiting for transfers between devices, body(): lax.psum_scatter(spread, ('section', 'dp'), scatter_dimension=0, tiled=True)  30.7 us
    all_gather x1, waiting for transfers between devices, body(): lax.all_gather(normed_rows, ('section', 'dp'), axis=0, tiled=True)  23.1 us
  transfers between devices with their start and end apart: 4, of which 4 were waited for; matrix products, arithmetic and copies ran while one was open for 2% of the time, Pallas kernels for 0%

commit v1 on v0

v1 whole, which is shorter than its diff:
```python
import functools
import jax
import jax.numpy as jnp
from jax import lax
from jax.experimental import pallas as pl
from jax.experimental.pallas import tpu as pltpu
from jax.sharding import Mesh, PartitionSpec as P

NSENT = 100
LIVE = 112
loss_scale = 8192.0
epsilon = 1e-06
f32, bf16 = jnp.float32, jnp.bfloat16


def shift(x, axis, k):
    n = lax.axis_size(axis)
    return lax.ppermute(x, axis, [(i, (i + k) % n) for i in range(n)])


def norm_kernel(y_ref, *refs):
    Y = len(refs) - 2
    blocks, out_ref, inv_ref = refs[:Y], refs[Y], refs[Y + 1]
    Z = blocks[0].shape[0]
    total = jnp.zeros((LIVE, 128), f32)
    for block in blocks:
        for z in range(Z):
            a = block[z, 0:LIVE, :].astype(f32)
            total = total + a * a
    mean_square = jnp.sum(total, axis=1, keepdims=True) / (Z * Y * 128)
    inv = lax.rsqrt(mean_square + epsilon)
    inv_ref[...] = inv
    for k, block in enumerate(blocks):
        y = lax.rem(y_ref[0] - k + Y, Y)
        for z in range(Z):
            a = block[z, 0:LIVE, :].astype(f32)
            pieces = block[z, LIVE:128, :].astype(f32)
            gain = pieces[0:1] + pieces[1:2] + pieces[2:3]
            at = pl.multiple_of((z * Y + y) * 128, 128)
            out_ref[:, pl.ds(at, 128)] = (a * inv * gain).astype(bf16)


def norm_rows(y, blocks):
    Y, Z = len(blocks), blocks[0].shape[0]
    vmem = pl.BlockSpec(memory_space=pltpu.VMEM)
    return pl.pallas_call(
        norm_kernel,
        out_shape=(
            jax.ShapeDtypeStruct((LIVE, Z * Y * 128), bf16),
            jax.ShapeDtypeStruct((LIVE, 1), f32),
        ),
        in_specs=[pl.BlockSpec(memory_space=pltpu.SMEM)] + [vmem] * Y,
        out_specs=(vmem, vmem),
        compiler_params=pltpu.CompilerParams(vmem_limit_bytes=32 << 20),
        name="norm_rows",
    )(y, *blocks)


def split_kernel(Y, y_ref, *refs):
    parts, outs = refs[:-Y], refs[-Y:]
    Z = outs[0].shape[0]
    for k, out in enumerate(outs):
        y = lax.rem(y_ref[0] + k, Y)
        for z in range(Z):
            at = pl.multiple_of((z * Y + y) * 128, 128)
            total = parts[0][:, pl.ds(at, 128)].astype(f32)
            for part in parts[1:]:
                total = total + part[:, pl.ds(at, 128)].astype(f32)
            out[z] = total.astype(out.dtype)


def split_rows(y, Y, parts):
    D = parts[0].shape[1]
    Z = D // (Y * 128)
    vmem = pl.BlockSpec(memory_space=pltpu.VMEM)
    return pl.pallas_call(
        functools.partial(split_kernel, Y),
        out_shape=tuple(
            jax.ShapeDtypeStruct((Z, LIVE, 128), f32 if k == 0 else bf16) for k in range(Y)
        ),
        in_specs=[pl.BlockSpec(memory_space=pltpu.SMEM)] + [vmem] * len(parts),
        out_specs=(vmem,) * Y,
        compiler_params=pltpu.CompilerParams(vmem_limit_bytes=32 << 20),
        name="split_rows",
    )(y, *parts)


def merge(stats, axis):
    top, total, weighted, target = (lax.index_in_dim(stats, i, axis + 1, False) for i in range(4))
    best = jnp.max(top, axis=axis, keepdims=True)
    scale = jnp.exp(top - best)
    return jnp.stack(
        [
            jnp.squeeze(best, axis),
            jnp.sum(total * scale, axis=axis),
            jnp.sum(weighted * scale, axis=axis),
            jnp.sum(target, axis=axis),
        ]
    )


def body(hidden, norm_gain, head_weight, targets, span_starts, live_rows):
    Z, Y, X = (lax.axis_size(a) for a in "zyx")
    V, D = head_weight.shape
    vocab = V * 2 * Z * Y * X
    c, z, y, x = (lax.axis_index(a) for a in "czyx")
    y_here = jnp.reshape(y, (1,))

    weight_other = shift(head_weight, "c", 1)
    weight = jnp.concatenate([head_weight, weight_other], axis=0)

    span_order = jnp.cumsum(span_starts) - 1
    sentinel_ids = vocab - 1 - jnp.clip(span_order, 0, NSENT - 1)
    labels = jnp.where(span_starts > 0, sentinel_ids, targets)
    meta = jnp.stack([labels, live_rows])
    meta = jnp.concatenate([meta, shift(meta, "c", 1)])
    metas = jnp.stack([meta] + [shift(meta, "x", k) for k in range(1, X)])[:, :, :LIVE]
    labels_all = metas[:, 0].reshape(-1)
    live_float = metas[:, 1].astype(f32).reshape(-1)
    live_total = jnp.sum(live_float) + jnp.sum(metas[:, 3].astype(f32))

    high = norm_gain.astype(bf16)
    rest = norm_gain - high.astype(f32)
    middle = rest.astype(bf16)
    low = (rest - middle.astype(f32)).astype(bf16)
    block = jnp.concatenate(
        [hidden[:LIVE], jnp.stack([high, middle, low]), jnp.zeros((128 - LIVE - 3, 128), bf16)]
    )
    block = lax.all_to_all(jnp.broadcast_to(block[None], (Z, 128, 128)), "z", 0, 0)
    blocks = [block] + [shift(block, "y", k) for k in range(1, Y)]
    normed, inv_rms = norm_rows(y_here, blocks)

    normed_all = jnp.concatenate([normed] + [shift(normed, "x", j) for j in range(1, X)])
    logits = jnp.einsum("rd,vd->rv", normed_all, weight, preferred_element_type=f32)
    place = (z * Y + y) * X + x
    columns = lax.iota(jnp.int32, V)
    columns = jnp.concatenate(
        [(c * (Z * Y * X) + place) * V + columns, ((1 - c) * (Z * Y * X) + place) * V + columns]
    )
    matches = labels_all[:, None] == columns[None, :]
    top = jnp.max(logits, axis=1)
    weights = jnp.exp(logits - top[:, None])
    stats = jnp.stack(
        [
            top,
            jnp.sum(weights, axis=1),
            jnp.sum(weights * logits, axis=1),
            jnp.sum(jnp.where(matches, logits, 0.0), axis=1),
        ]
    ).reshape(4, X, LIVE)
    stats = lax.all_to_all(jnp.broadcast_to(stats[None], (Z * Y, 4, X, LIVE)), ("z", "y"), 0, 0)
    stats = merge(stats, 0)
    stats = merge(
        jnp.stack([stats] + [jnp.roll(shift(stats, "x", k), k, axis=1) for k in range(1, X)]), 0
    )
    row_max, exp_total, weighted_total, target_logit = (s.reshape(-1) for s in stats)
    log_total = row_max + jnp.log(exp_total)
    loss = jnp.sum(live_float * (log_total - target_logit))
    mean_loss = (loss + shift(loss, "c", 1)) / live_total

    row_factor = live_float * (loss_scale / live_total)
    probability = jnp.exp(logits - log_total[:, None])
    grad_logits = ((probability - matches.astype(f32)) * row_factor[:, None]).astype(bf16)
    parts = [
        jnp.dot(grad_logits[j * LIVE : (j + 1) * LIVE], weight, preferred_element_type=f32).astype(bf16)
        for j in range(X)
    ]
    arrived = [shift(parts[j], "x", -j) for j in range(1, X)]
    outs = split_rows(y_here, Y, [parts[0]] + arrived)
    total = outs[0]
    for k in range(1, Y):
        total = total + shift(outs[k], "y", k).astype(f32)
    total = lax.all_to_all(total.astype(bf16), "z", 0, 0)
    normed_grad = jnp.sum(total.astype(f32), axis=0)

    grad_t = functools.partial(jnp.einsum, "rv,rd->vd", preferred_element_type=f32)
    weight_grad_other = grad_t(grad_logits[:, V:], normed_all).astype(bf16)
    weight_grad = grad_t(grad_logits[:, :V], normed_all)
    weight_grad = (weight_grad + shift(weight_grad_other, "c", 1).astype(f32)).astype(bf16)

    activation = hidden[:LIVE].astype(f32)
    inner = row_factor[:LIVE] * (weighted_total[:LIVE] / exp_total[:LIVE] - target_logit[:LIVE])
    scaled = normed_grad * norm_gain[None, :]
    hidden_grad = inv_rms * scaled - activation * (inv_rms * inv_rms * (inner[:, None] / D))
    hidden_grad = jnp.pad(hidden_grad.astype(bf16), ((0, 128 - LIVE), (0, 0)))

    gain_grad = jnp.sum(normed_grad * activation * inv_rms, axis=0)
    gain_grad = gain_grad + shift(gain_grad, "c", 1)
    gain_grad = gain_grad + sum(shift(gain_grad, "x", k) for k in range(1, X))
    return (hidden_grad, gain_grad, weight_grad, mean_loss)


def solution(mesh):
    S, T, X = mesh.devices.shape
    Y = 4 if T % 4 == 0 else 2
    split = Mesh(mesh.devices.reshape(S, T // Y, Y, X), ("c", "z", "y", "x"))
    return jax.shard_map(
        body,
        mesh=split,
        in_specs=(
            P(("c", "x"), ("z", "y")),
            P(("z", "y")),
            P(("c", "z", "y", "x"), None),
            P(("c", "x")),
            P(("c", "x")),
            P(("c", "x")),
        ),
        out_specs=(
            P(("c", "x"), ("z", "y")),
            P(("z", "y")),
            P(("c", "z", "y", "x"), None),
            P(),
        ),
        check_vma=False,
    )
```

time: 754 us -> 254 us (0.34); the launches traced: 741 us -> 254 us
  blocking collectives: 321 us -> 15.5 us
  waiting for transfers between devices: 366 us -> 141 us
  starting transfers between devices: 0.16 us -> 43.7 us
  local copies, waits for them, and re-layouts: 0.79 us -> 14.6 us
  between operations: 17 us -> 4.77 us
    reduce_scatter x2 -> x0, waiting for transfers between devices: 267 us -> none  [the longest x1 236 us: body(): lax.psum_scatter(partial_value, 'tensor', scatter_dimension=1, tiled=True)]
    psum x4 -> x0, blocking collectives: 214 us -> none  [the longest x1 74.5 us: body(): lax.psum((jnp.sum(jnp.exp(logits - row_max[:, None]), axis=1), own_target...]
    ppermute x0 -> x26, waiting for transfers between devices: none -> 121 us  [shift(): return lax.ppermute(x, axis, [(i, (i + k) % n) for i in range(n)])]
    all_gather x2 -> x0, waiting for transfers between devices: 99 us -> none  [the longest x1 75.9 us: body(): normed_rows = lax.all_gather(normed_part, 'tensor', axis=1, tiled=True)]
    pmax x1 -> x0, blocking collectives: 76 us -> none  [body(): row_max = lax.pmax(local_max, ('section', 'tensor', 'dp'))]
    ppermute x0 -> x26, starting transfers between devices: none -> 33.9 us  [shift(): return lax.ppermute(x, axis, [(i, (i + k) % n) for i in range(n)])]
    all_gather x2 -> x0, blocking collectives: 31.3 us -> none  [the longest x1 18.6 us: body(): lax.all_gather(live_rows, ('section', 'dp'), axis=0, tiled=True)]
    all_to_all x0 -> x2, waiting for transfers between devices: none -> 20.4 us  [the longest x1 10.7 us: body(): total = lax.all_to_all(total.astype(bf16), 'z', 0, 0)]
  transfers between devices with their start and end apart: 4 -> 28, of which waited for: 4 -> 17; matrix products, arithmetic and copies ran while one was open for 2% -> 7% of each run, Pallas kernels for 0% -> 1%
where the time goes in v1:
time: 254 us
  waiting for transfers between devices  141 us (56%)
  starting transfers between devices  43.7 us (17%)
  matrix products  26.3 us (10%)
  blocking collectives  15.5 us (6%)
  local copies, waits for them, and re-layouts  14.6 us (6%)
  other arithmetic  6.23 us (2%)
  between operations  4.77 us (2%)
    ppermute x26, waiting for transfers between devices, shift(): return lax.ppermute(x, axis, [(i, (i + k) % n) for i in range(n)])  121 us
    ppermute x26, starting transfers between devices, shift(): return lax.ppermute(x, axis, [(i, (i + k) % n) for i in range(n)])  33.9 us
    all_to_all x1, blocking collectives, body(): lax.all_to_all(jnp.broadcast_to(stats[None], (Z * Y, 4, X, LIVE)), ('z',...  15.5 us
    all_to_all x1, waiting for transfers between devices, body(): total = lax.all_to_all(total.astype(bf16), 'z', 0, 0)  10.7 us
    all_to_all x1, waiting for transfers between devices, body(): lax.all_to_all(jnp.broadcast_to(block[None], (Z, 128, 128)), 'z', 0, 0)  9.68 us
    dot_general x1, matrix products, body(): weight_grad = grad_t(grad_logits[:, :V], normed_all)  7.72 us
    dot_general x1, matrix products, body(): jnp.einsum('rd,vd->rv', normed_all, weight, preferred_element_type=f32)  6.74 us
    dot_general x1, matrix products, body(): weight_grad_other = grad_t(grad_logits[:, V:], normed_all).astype(bf16)  6.67 us
  transfers between devices with their start and end apart: 28, of which 17 were waited for; matrix products, arithmetic and copies ran while one was open for 7% of the time, Pallas kernels for 1%

profile of v1, /device:TPU:1, one launch (start us, length us, event | category | flops | bytes accessed | tf_op | source)
XLA Modules:
  0.0 253.7 jit_solution(4928241891835380983)
XLA Ops:
  0.6 3.3 %collective-permute-start.6 = (bf16[512,4096]{1,0:T(8,128)(2,1)}, bf16[512,4096]{1,0:T(8,128)(2,1)}, u32[]{:S(2)}, u32[]{:S(2)}) collective-permute-start(bf16[512,4096]{1,0:T(8,128)(2,1)} %param.8), channel_id=1, source_target_pairs={{0,128},{128,0},{1,129},{129,1},{2,130},{130,2},{3,131},{131,3},{4... | collective-permute-start | bytes 12582920 | tf_op jit(solution)/shard_map/ppermute | solution.py:18
  4.0 0.8 slice.101
  4.7 0.7 convert_bitcast_fusion
  5.6 0.7 broadcast_in_dim.15
  6.3 6.5 %all-to-all-start = ((bf16[8,128,128]{2,1,0:T(8,128)(2,1)}), bf16[8,128,128]{2,1,0:T(8,128)(2,1)S(1)}, u32[]{:S(2)}, u32[]{:S(2)}) async-start(bf16[8,128,128]{2,1,0:T(8,128)(2,1)} %broadcast_in_dim.15), calls=%async_computation | async-start | bytes 524288 | tf_op jit(solution)/shard_map/all_to_all | solution.py:129
  12.8 0.8 copy.29
  13.8 0.7 fusion.28
  14.5 0.7 pad_add_fusion.6
  15.5 9.7 %all-to-all-done.refs_0_ = bf16[8,128,128]{2,1,0:T(8,128)(2,1)S(1)} async-done(((bf16[8,128,128]{2,1,0:T(8,128)(2,1)}), bf16[8,128,128]{2,1,0:T(8,128)(2,1)S(1)}, u32[]{:S(2)}, u32[]{:S(2)}) %all-to-all-start) | async-done | bytes 262176 | tf_op jit(solution)/shard_map/all_to_all | solution.py:129
  25.2 1.3 collective-permute-start
  26.5 2.6 %collective-permute-start.1 = (bf16[8,128,128]{2,1,0:T(8,128)(2,1)S(1)}, bf16[8,128,128]{2,1,0:T(8,128)(2,1)S(1)}, u32[]{:S(2)}, u32[]{:S(2)}) collective-permute-start(bf16[8,128,128]{2,1,0:T(8,128)(2,1)S(1)} %all-to-all-done.refs_0_), channel_id=1, source_target_pairs={{0,8},{4,12},{8,0},{12,4},{1,9},{5,13},{9,1},{13,5},{2,10},{6,14},... | collective-permute-start | bytes 786440 | tf_op jit(solution)/shard_map/ppermute | solution.py:18
  29.1 1.1 collective-permute-start.2
  30.1 4.6 %constant_dynamic-update-slice_fusion.5 = bf16[1024,4096]{1,0:T(8,128)(2,1)} fusion(bf16[512,4096]{1,0:T(8,128)(2,1)} %param.8), kind=kLoop, calls=%fused_computation.47 | loop fusion | bytes 8388608
  34.8 5.9 %collective-permute-done.1.refs_2_ = bf16[8,128,128]{2,1,0:T(8,128)(2,1)S(1)} collective-permute-done((bf16[8,128,128]{2,1,0:T(8,128)(2,1)S(1)}, bf16[8,128,128]{2,1,0:T(8,128)(2,1)S(1)}, u32[]{:S(2)}, u32[]{:S(2)}) %collective-permute-start.1) | collective-permute-done | bytes 262176 | tf_op jit(solution)/shard_map/ppermute | solution.py:18
  40.6 0.5 norm_rows.1
  41.1 1.3 collective-permute-start.3
  42.5 1.5 collective-permute-start.10
  44.0 1.5 collective-permute-start.9
  45.5 0.3 collective-permute-start.8
  45.9 17.8 %collective-permute-done.9 = s32[4,128]{1,0:T(4,128)S(1)} collective-permute-done((s32[4,128]{1,0:T(4,128)S(1)}, s32[4,128]{1,0:T(4,128)S(1)}, u32[]{:S(2)}, u32[]{:S(2)}) %collective-permute-start.9) | collective-permute-done | bytes 2080 | tf_op jit(solution)/shard_map/ppermute | solution.py:18
  63.8 0.9 collective-permute-start.4
  64.7 0.9 collective-permute-start.5
  65.7 18.9 %collective-permute-done.4 = bf16[112,4096]{1,0:T(8,128)(2,1)S(1)} collective-permute-done((bf16[112,4096]{1,0:T(8,128)(2,1)S(1)}, bf16[112,4096]{1,0:T(8,128)(2,1)S(1)}, u32[]{:S(2)}, u32[]{:S(2)}) %collective-permute-start.4) | collective-permute-done | bytes 917536 | tf_op jit(solution)/shard_map/ppermute | solution.py:18
  84.7 19.8 %collective-permute-done.5 = bf16[112,4096]{1,0:T(8,128)(2,1)S(1)} collective-permute-done((bf16[112,4096]{1,0:T(8,128)(2,1)S(1)}, bf16[112,4096]{1,0:T(8,128)(2,1)S(1)}, u32[]{:S(2)}, u32[]{:S(2)}) %collective-permute-start.5) | collective-permute-done | bytes 917536 | tf_op jit(solution)/shard_map/ppermute | solution.py:18
  104.6 6.0 %constant_dynamic-update-slice_fusion.4 = bf16[1024,4096]{1,0:T(8,128)(2,1)} fusion(bf16[1024,4096]{1,0:T(8,128)(2,1)} %constant_dynamic-update-slice_fusion.5, bf16[512,4096]{1,0:T(8,128)(2,1)} %collective-permute-done.6), kind=kLoop, calls=%fused_computation.46 | loop fusion | bytes 8388608 | tf_op jit(solution)/shard_map/concatenate | solution.py:110
  110.5 6.7 %fusion.34 = (f32[448]{0:T(512)S(1)}, f32[448,1024]{1,0:T(8,128)S(1)}) fusion(bf16[448,4096]{1,0:T(8,128)(2,1)S(1)} %constant_dynamic-update-slice_fusion, bf16[1024,4096]{1,0:T(8,128)(2,1)} %constant_dynamic-update-slice_fusion.4), kind=kOutput, calls=%fused_computation.92 | convolution fusion | flops 3758554624 | bytes 13895424 | tf_op jit(solution)/shard_map/rd,vd->rv/dot_general | solution.py:134
  117.4 0.9 fusion.4
  118.6 15.5 %all_to_all.15 = f32[32,4,4,112]{3,2,1,0:T(4,128)S(1)} all-to-all(f32[32,4,4,112]{3,2,1,0:T(4,128)S(1)} %broadcast_in_dim.34), channel_id=1, replica_groups=mesh['c'=2,'z'=8,'y'=4,'x'=4] {'z','y'}, dimensions={0} | all-to-all | bytes 458752 | tf_op jit(solution)/shard_map/all_to_all | solution.py:151
  134.3 4.6 %collective-permute-start.13 = (f32[4,4,112]{2,1,0:T(4,128)S(1)}, f32[4,4,112]{2,1,0:T(4,128)S(1)}, u32[]{:S(2)}, u32[]{:S(2)}) collective-permute-start(f32[4,4,112]{2,1,0:T(4,128)S(1)} %get-tuple-element.33), channel_id=1, source_target_pairs={{0,3},{1,0},{2,1},{3,2},{4,7},{5,4},{6,5},{7,6},{8,11},{9,8},{10,9... | collective-permute-start | bytes 21512 | tf_op jit(solution)/shard_map/ppermute | solution.py:18
  138.8 0.5 collective-permute-start.12
  139.6 3.2 %collective-permute-done.12 = f32[4,4,112]{2,1,0:T(4,128)S(1)} collective-permute-done((f32[4,4,112]{2,1,0:T(4,128)S(1)}, f32[4,4,112]{2,1,0:T(4,128)S(1)}, u32[]{:S(2)}, u32[]{:S(2)}) %collective-permute-start.12) | collective-permute-done | bytes 7200 | tf_op jit(solution)/shard_map/ppermute | solution.py:18
  143.2 0.6 fusion.27
  145.3 0.5 fusion.3
  145.8 6.7 %convolution_convert_fusion = bf16[512,4096]{1,0:T(8,128)(2,1)} fusion(bf16[448,4096]{1,0:T(8,128)(2,1)} %copy-done.1, bf16[448,1024]{1,0:T(8,128)(2,1)S(1)} %fusion.3), kind=kOutput, calls=%fused_computation.1 | convolution fusion | flops 1881145344 | bytes 8323072 | tf_op jit(solution)/shard_map/rv,rd->vd/dot_general | solution.py:177
  152.5 4.0 %collective-permute-start.24 = (bf16[512,4096]{1,0:T(8,128)(2,1)}, bf16[512,4096]{1,0:T(8,128)(2,1)}, u32[]{:S(2)}, u32[]{:S(2)}) collective-permute-start(bf16[512,4096]{1,0:T(8,128)(2,1)} %convolution_convert_fusion), channel_id=1, source_target_pairs={{0,128},{128,0},{1,129},{129,1},{2,130},{130,2},{3,131},{131,3},{4... | collective-permute-start | bytes 12582920 | tf_op jit(solution)/shard_map/ppermute | solution.py:18
  156.5 1.3 convolution_convert_fusion.3
  157.8 1.3 convolution_convert_fusion.2
  159.1 1.3 convolution_convert_fusion.1
  160.5 1.3 collective-permute-start.15
  161.8 0.8 collective-permute-start.16
  162.6 1.3 convolution_convert_fusion.4.refs_0_
  164.0 18.4 %collective-permute-done.14.refs_1_ = bf16[112,4096]{1,0:T(8,128)(2,1)S(1)} collective-permute-done((bf16[112,4096]{1,0:T(8,128)(2,1)S(1)}, bf16[112,4096]{1,0:T(8,128)(2,1)S(1)}, u32[]{:S(2)}, u32[]{:S(2)}) %collective-permute-start.14) | collective-permute-done | bytes 917536 | tf_op jit(solution)/shard_map/ppermute | solution.py:18
  182.4 1.6 collective-permute-done.15.refs_2_
  184.1 20.0 %collective-permute-done.16.refs_3_ = bf16[112,4096]{1,0:T(8,128)(2,1)S(1)} collective-permute-done((bf16[112,4096]{1,0:T(8,128)(2,1)S(1)}, bf16[112,4096]{1,0:T(8,128)(2,1)S(1)}, u32[]{:S(2)}, u32[]{:S(2)}) %collective-permute-start.16) | collective-permute-done | bytes 917536 | tf_op jit(solution)/shard_map/ppermute | solution.py:18
  204.0 0.9 split_rows.1
  205.0 1.3 collective-permute-start.19
  206.3 0.6 collective-permute-start.18
  206.8 0.5 collective-permute-start.17
  207.4 4.4 %collective-permute-done.19 = bf16[8,112,128]{2,1,0:T(8,128)(2,1)S(1)} collective-permute-done((bf16[8,112,128]{2,1,0:T(8,128)(2,1)S(1)}, bf16[8,112,128]{2,1,0:T(8,128)(2,1)S(1)}, u32[]{:S(2)}, u32[]{:S(2)}) %collective-permute-start.19) | collective-permute-done | bytes 229408 | tf_op jit(solution)/shard_map/ppermute | solution.py:18
  211.8 2.4 collective-permute-done.18
  214.2 6.0 %collective-permute-done.17 = bf16[8,112,128]{2,1,0:T(8,128)(2,1)S(1)} collective-permute-done((bf16[8,112,128]{2,1,0:T(8,128)(2,1)S(1)}, bf16[8,112,128]{2,1,0:T(8,128)(2,1)S(1)}, u32[]{:S(2)}, u32[]{:S(2)}) %collective-permute-start.17) | collective-permute-done | bytes 229408 | tf_op jit(solution)/shard_map/ppermute | solution.py:18
  220.2 0.8 add_convert_fusion.1
  221.0 3.4 %all-to-all-start.2 = ((bf16[8,112,128]{2,1,0:T(8,128)(2,1)}), bf16[8,112,128]{2,1,0:T(8,128)(2,1)S(1)}, u32[]{:S(2)}, u32[]{:S(2)}) async-start(bf16[8,112,128]{2,1,0:T(8,128)(2,1)} %add_convert_fusion.1), calls=%async_computation.2 | async-start | bytes 458752 | tf_op jit(solution)/shard_map/all_to_all | solution.py:173
  224.6 10.7 %all-to-all-done.2 = bf16[8,112,128]{2,1,0:T(8,128)(2,1)S(1)} async-done(((bf16[8,112,128]{2,1,0:T(8,128)(2,1)}), bf16[8,112,128]{2,1,0:T(8,128)(2,1)S(1)}, u32[]{:S(2)}, u32[]{:S(2)}) %all-to-all-start.2) | async-done | bytes 229408 | tf_op jit(solution)/shard_map/all_to_all | solution.py:173
  235.5 1.1 collective-permute-start.20
  236.7 0.8 collective-permute-done.20
  237.5 0.5 collective-permute-start.23
  238.0 1.0 collective-permute-start.21
  239.0 1.3 collective-permute-start.22
  240.2 1.1 collective-permute-start.25
  241.4 1.0 collective-permute-done.25
  243.7 0.6 pad.4
  244.3 0.5 add_add_fusion
  244.9 7.7 %add_convert_fusion = bf16[512,4096]{1,0:T(8,128)(2,1)} fusion(bf16[512,4096]{1,0:T(8,128)(2,1)} %collective-permute-done.24, bf16[448,4096]{1,0:T(8,128)(2,1)} %copy-done.1, bf16[448,1024]{1,0:T(8,128)(2,1)S(1)} %fusion.3), kind=kOutput, calls=%fused_computation | convolution fusion | flops 1885339648 | bytes 12517376 | tf_op jit(solution)/shard_map/rv,rd->vd/dot_general | solution.py:178
  (69 shorter events, 2.9 us)
Async XLA Ops:
  0.6 103.9 %collective-permute-start.6 = (bf16[512,4096]{1,0:T(8,128)(2,1)}, bf16[512,4096]{1,0:T(8,128)(2,1)}, u32[]{:S(2)}, u32[]{:S(2)}) collective-permute-start(bf16[512,4096]{1,0:T(8,128)(2,1)} %param.8), channel_id=1, source_target_pairs={{0,128},{128,0},{1,129},{129,1},{2,130},{130,2},{3,131},{131,3},{4... | collective-permute-start | bytes 12582920 | tf_op jit(solution)/shard_map/ppermute | solution.py:18
  6.3 18.8 %all-to-all-start = ((bf16[8,128,128]{2,1,0:T(8,128)(2,1)}), bf16[8,128,128]{2,1,0:T(8,128)(2,1)S(1)}, u32[]{:S(2)}, u32[]{:S(2)}) async-start(bf16[8,128,128]{2,1,0:T(8,128)(2,1)} %broadcast_in_dim.15), calls=%async_computation | async-start | bytes 524288 | tf_op jit(solution)/shard_map/all_to_all | solution.py:129
  15.2 27.3 %copy-start.4 = (s32[128]{0:T(128)S(1)}, s32[128]{0:T(128)}, u32[]{:S(2)}) copy-start(s32[128]{0:T(128)} %param.11) | copy-start | bytes 1540
  15.2 27.3 %collective-permute-start.7 = (s32[2,128]{1,0:T(2,128)S(1)}, s32[2,128]{1,0:T(2,128)S(1)}, u32[]{:S(2)}, u32[]{:S(2)}) collective-permute-start(s32[2,128]{1,0:T(2,128)S(1)} %pad_add_fusion.6), channel_id=1, source_target_pairs={{0,128},{128,0},{1,129},{129,1},{2,130},{130,2},{3,131},{131,3},{4... | collective-permute-start | bytes 3080 | tf_op jit(solution)/shard_map/ppermute | solution.py:18
  25.2 9.6 %collective-permute-start = (bf16[8,128,128]{2,1,0:T(8,128)(2,1)S(1)}, bf16[8,128,128]{2,1,0:T(8,128)(2,1)S(1)}, u32[]{:S(2)}, u32[]{:S(2)}) collective-permute-start(bf16[8,128,128]{2,1,0:T(8,128)(2,1)S(1)} %all-to-all-done.refs_0_), channel_id=1, source_target_pairs={{0,4},{4,8},{8,12},{12,0},{1,5},{5,9},{9,13},{13,1},{2,6},{6,10},{... | collective-permute-start | bytes 786440 | tf_op jit(solution)/shard_map/ppermute | solution.py:18
  26.5 14.2 %collective-permute-start.1 = (bf16[8,128,128]{2,1,0:T(8,128)(2,1)S(1)}, bf16[8,128,128]{2,1,0:T(8,128)(2,1)S(1)}, u32[]{:S(2)}, u32[]{:S(2)}) collective-permute-start(bf16[8,128,128]{2,1,0:T(8,128)(2,1)S(1)} %all-to-all-done.refs_0_), channel_id=1, source_target_pairs={{0,8},{4,12},{8,0},{12,4},{1,9},{5,13},{9,1},{13,5},{2,10},{6,14},... | collective-permute-start | bytes 786440 | tf_op jit(solution)/shard_map/ppermute | solution.py:18
  29.1 11.6 %collective-permute-start.2 = (bf16[8,128,128]{2,1,0:T(8,128)(2,1)S(1)}, bf16[8,128,128]{2,1,0:T(8,128)(2,1)S(1)}, u32[]{:S(2)}, u32[]{:S(2)}) collective-permute-start(bf16[8,128,128]{2,1,0:T(8,128)(2,1)S(1)} %all-to-all-done.refs_0_), channel_id=1, source_target_pairs={{0,12},{4,0},{8,4},{12,8},{1,13},{5,1},{9,5},{13,9},{2,14},{6,2},{... | collective-permute-start | bytes 786440 | tf_op jit(solution)/shard_map/ppermute | solution.py:18
  41.1 24.5 %collective-permute-start.3 = (bf16[112,4096]{1,0:T(8,128)(2,1)S(1)}, bf16[112,4096]{1,0:T(8,128)(2,1)S(1)}, u32[]{:S(2)}, u32[]{:S(2)}) collective-permute-start(bf16[112,4096]{1,0:T(8,128)(2,1)S(1)} %get-tuple-element.11), channel_id=1, source_target_pairs={{0,1},{1,2},{2,3},{3,0},{4,5},{5,6},{6,7},{7,4},{8,9},{9,10},{10,1... | collective-permute-start | bytes 2752520 | tf_op jit(solution)/shard_map/ppermute | solution.py:18
  42.5 3.4 %collective-permute-start.10 = (s32[4,128]{1,0:T(4,128)S(1)}, s32[4,128]{1,0:T(4,128)S(1)}, u32[]{:S(2)}, u32[]{:S(2)}) collective-permute-start(s32[4,128]{1,0:T(4,128)S(1)} %pad_add_fusion.5), channel_id=1, source_target_pairs={{0,3},{1,0},{2,1},{3,2},{4,7},{5,4},{6,5},{7,6},{8,11},{9,8},{10,9... | collective-permute-start | bytes 6152 | tf_op jit(solution)/shard_map/ppermute | solution.py:18
  44.0 19.7 %collective-permute-start.9 = (s32[4,128]{1,0:T(4,128)S(1)}, s32[4,128]{1,0:T(4,128)S(1)}, u32[]{:S(2)}, u32[]{:S(2)}) collective-permute-start(s32[4,128]{1,0:T(4,128)S(1)} %pad_add_fusion.5), channel_id=1, source_target_pairs={{0,2},{1,3},{2,0},{3,1},{4,6},{5,7},{6,4},{7,5},{8,10},{9,11},{10,... | collective-permute-start | bytes 6152 | tf_op jit(solution)/shard_map/ppermute | solution.py:18
  45.5 18.2 %collective-permute-start.8 = (s32[4,128]{1,0:T(4,128)S(1)}, s32[4,128]{1,0:T(4,128)S(1)}, u32[]{:S(2)}, u32[]{:S(2)}) collective-permute-start(s32[4,128]{1,0:T(4,128)S(1)} %pad_add_fusion.5), channel_id=1, source_target_pairs={{0,1},{1,2},{2,3},{3,0},{4,5},{5,6},{6,7},{7,4},{8,9},{9,10},{10,1... | collective-permute-start | bytes 6152 | tf_op jit(solution)/shard_map/ppermute | solution.py:18
  63.8 20.8 %collective-permute-start.4 = (bf16[112,4096]{1,0:T(8,128)(2,1)S(1)}, bf16[112,4096]{1,0:T(8,128)(2,1)S(1)}, u32[]{:S(2)}, u32[]{:S(2)}) collective-permute-start(bf16[112,4096]{1,0:T(8,128)(2,1)S(1)} %get-tuple-element.11), channel_id=1, source_target_pairs={{0,2},{1,3},{2,0},{3,1},{4,6},{5,7},{6,4},{7,5},{8,10},{9,11},{10,... | collective-permute-start | bytes 2752520 | tf_op jit(solution)/shard_map/ppermute | solution.py:18
  64.7 39.8 %collective-permute-start.5 = (bf16[112,4096]{1,0:T(8,128)(2,1)S(1)}, bf16[112,4096]{1,0:T(8,128)(2,1)S(1)}, u32[]{:S(2)}, u32[]{:S(2)}) collective-permute-start(bf16[112,4096]{1,0:T(8,128)(2,1)S(1)} %get-tuple-element.11), channel_id=1, source_target_pairs={{0,3},{1,0},{2,1},{3,2},{4,7},{5,4},{6,5},{7,6},{8,11},{9,8},{10,9... | collective-permute-start | bytes 2752520 | tf_op jit(solution)/shard_map/ppermute | solution.py:18
  104.5 6.0 %copy-start.1 = (bf16[448,4096]{1,0:T(8,128)(2,1)}, bf16[448,4096]{1,0:T(8,128)(2,1)S(1)}, u32[]{:S(2)}) copy-start(bf16[448,4096]{1,0:T(8,128)(2,1)S(1)} %constant_dynamic-update-slice_fusion) | copy-start | bytes 11010052
  134.3 5.4 %collective-permute-start.13 = (f32[4,4,112]{2,1,0:T(4,128)S(1)}, f32[4,4,112]{2,1,0:T(4,128)S(1)}, u32[]{:S(2)}, u32[]{:S(2)}) collective-permute-start(f32[4,4,112]{2,1,0:T(4,128)S(1)} %get-tuple-element.33), channel_id=1, source_target_pairs={{0,3},{1,0},{2,1},{3,2},{4,7},{5,4},{6,5},{7,6},{8,11},{9,8},{10,9... | collective-permute-start | bytes 21512 | tf_op jit(solution)/shard_map/ppermute | solution.py:18
  138.8 4.0 %collective-permute-start.12 = (f32[4,4,112]{2,1,0:T(4,128)S(1)}, f32[4,4,112]{2,1,0:T(4,128)S(1)}, u32[]{:S(2)}, u32[]{:S(2)}) collective-permute-start(f32[4,4,112]{2,1,0:T(4,128)S(1)} %get-tuple-element.33), channel_id=1, source_target_pairs={{0,2},{1,3},{2,0},{3,1},{4,6},{5,7},{6,4},{7,5},{8,10},{9,11},{10,... | collective-permute-start | bytes 21512 | tf_op jit(solution)/shard_map/ppermute | solution.py:18
  139.4 3.7 %collective-permute-start.11 = (f32[4,4,112]{2,1,0:T(4,128)S(1)}, f32[4,4,112]{2,1,0:T(4,128)S(1)}, u32[]{:S(2)}, u32[]{:S(2)}) collective-permute-start(f32[4,4,112]{2,1,0:T(4,128)S(1)} %get-tuple-element.33), channel_id=1, source_target_pairs={{0,1},{1,2},{2,3},{3,0},{4,5},{5,6},{6,7},{7,4},{8,9},{9,10},{10,1... | collective-permute-start | bytes 21512 | tf_op jit(solution)/shard_map/ppermute | solution.py:18
  145.3 11.2 %copy-start = (bf16[1024,4096]{1,0:T(8,128)(2,1)S(1)}, bf16[1024,4096]{1,0:T(8,128)(2,1)}, u32[]{:S(2)}) copy-start(bf16[1024,4096]{1,0:T(8,128)(2,1)} %constant_dynamic-update-slice_fusion.4) | copy-start | bytes 25165828
  152.5 92.4 %collective-permute-start.24 = (bf16[512,4096]{1,0:T(8,128)(2,1)}, bf16[512,4096]{1,0:T(8,128)(2,1)}, u32[]{:S(2)}, u32[]{:S(2)}) collective-permute-start(bf16[512,4096]{1,0:T(8,128)(2,1)} %convolution_convert_fusion), channel_id=1, source_target_pairs={{0,128},{128,0},{1,129},{129,1},{2,130},{130,2},{3,131},{131,3},{4... | collective-permute-start | bytes 12582920 | tf_op jit(solution)/shard_map/ppermute | solution.py:18
  160.4 22.0 %collective-permute-start.14 = (bf16[112,4096]{1,0:T(8,128)(2,1)S(1)}, bf16[112,4096]{1,0:T(8,128)(2,1)S(1)}, u32[]{:S(2)}, u32[]{:S(2)}) collective-permute-start(bf16[112,4096]{1,0:T(8,128)(2,1)S(1)} %convolution_convert_fusion.3), channel_id=1, source_target_pairs={{0,3},{1,0},{2,1},{3,2},{4,7},{5,4},{6,5},{7,6},{8,11},{9,8},{10,9... | collective-permute-start | bytes 2752520 | tf_op jit(solution)/shard_map/ppermute | solution.py:18
  160.5 23.6 %collective-permute-start.15 = (bf16[112,4096]{1,0:T(8,128)(2,1)S(1)}, bf16[112,4096]{1,0:T(8,128)(2,1)S(1)}, u32[]{:S(2)}, u32[]{:S(2)}) collective-permute-start(bf16[112,4096]{1,0:T(8,128)(2,1)S(1)} %convolution_convert_fusion.2), channel_id=1, source_target_pairs={{0,2},{1,3},{2,0},{3,1},{4,6},{5,7},{6,4},{7,5},{8,10},{9,11},{10,... | collective-permute-start | bytes 2752520 | tf_op jit(solution)/shard_map/ppermute | solution.py:18
  161.8 42.2 %collective-permute-start.16 = (bf16[112,4096]{1,0:T(8,128)(2,1)S(1)}, bf16[112,4096]{1,0:T(8,128)(2,1)S(1)}, u32[]{:S(2)}, u32[]{:S(2)}) collective-permute-start(bf16[112,4096]{1,0:T(8,128)(2,1)S(1)} %convolution_convert_fusion.1), channel_id=1, source_target_pairs={{0,1},{1,2},{2,3},{3,0},{4,5},{5,6},{6,7},{7,4},{8,9},{9,10},{10,1... | collective-permute-start | bytes 2752520 | tf_op jit(solution)/shard_map/ppermute | solution.py:18
  163.9 71.5 %copy-start.2 = (bf16[128,128]{1,0:T(8,128)(2,1)S(1)}, bf16[128,128]{1,0:T(8,128)(2,1)}, u32[]{:S(2)}) copy-start(bf16[128,128]{1,0:T(8,128)(2,1)} %param.6) | copy-start | bytes 98308
  164.0 71.5 %copy-start.3 = (f32[128]{0:T(128)S(1)}, f32[128]{0:T(128)}, u32[]{:S(2)}) copy-start(f32[128]{0:T(128)} %param.7) | copy-start | bytes 1540
  205.0 6.8 %collective-permute-start.19 = (bf16[8,112,128]{2,1,0:T(8,128)(2,1)S(1)}, bf16[8,112,128]{2,1,0:T(8,128)(2,1)S(1)}, u32[]{:S(2)}, u32[]{:S(2)}) collective-permute-start(bf16[8,112,128]{2,1,0:T(8,128)(2,1)S(1)} %get-tuple-element.15), channel_id=1, source_target_pairs={{0,12},{4,0},{8,4},{12,8},{1,13},{5,1},{9,5},{13,9},{2,14},{6,2},{... | collective-permute-start | bytes 688136 | tf_op jit(solution)/shard_map/ppermute | solution.py:18
  206.3 7.9 %collective-permute-start.18 = (bf16[8,112,128]{2,1,0:T(8,128)(2,1)S(1)}, bf16[8,112,128]{2,1,0:T(8,128)(2,1)S(1)}, u32[]{:S(2)}, u32[]{:S(2)}) collective-permute-start(bf16[8,112,128]{2,1,0:T(8,128)(2,1)S(1)} %get-tuple-element.14), channel_id=1, source_target_pairs={{0,8},{4,12},{8,0},{12,4},{1,9},{5,13},{9,1},{13,5},{2,10},{6,14},... | collective-permute-start | bytes 688136 | tf_op jit(solution)/shard_map/ppermute | solution.py:18
  206.8 13.4 %collective-permute-start.17 = (bf16[8,112,128]{2,1,0:T(8,128)(2,1)S(1)}, bf16[8,112,128]{2,1,0:T(8,128)(2,1)S(1)}, u32[]{:S(2)}, u32[]{:S(2)}) collective-permute-start(bf16[8,112,128]{2,1,0:T(8,128)(2,1)S(1)} %get-tuple-element.13), channel_id=1, source_target_pairs={{0,4},{4,8},{8,12},{12,0},{1,5},{5,9},{9,13},{13,1},{2,6},{6,10},{... | collective-permute-start | bytes 688136 | tf_op jit(solution)/shard_map/ppermute | solution.py:18
  221.0 14.4 %all-to-all-start.2 = ((bf16[8,112,128]{2,1,0:T(8,128)(2,1)}), bf16[8,112,128]{2,1,0:T(8,128)(2,1)S(1)}, u32[]{:S(2)}, u32[]{:S(2)}) async-start(bf16[8,112,128]{2,1,0:T(8,128)(2,1)} %add_convert_fusion.1), calls=%async_computation.2 | async-start | bytes 458752 | tf_op jit(solution)/shard_map/all_to_all | solution.py:173
  235.5 2.0 collective-permute-start.20
  237.5 6.8 %collective-permute-start.23 = (f32[128]{0:T(128)S(1)}, f32[128]{0:T(128)S(1)}, u32[]{:S(2)}, u32[]{:S(2)}) collective-permute-start(f32[128]{0:T(128)S(1)} %add.90), channel_id=1, source_target_pairs={{0,3},{1,0},{2,1},{3,2},{4,7},{5,4},{6,5},{7,6},{8,11},{9,8},{10,9... | collective-permute-start | bytes 1544 | tf_op jit(solution)/shard_map/ppermute | solution.py:18
  238.0 6.3 %collective-permute-start.21 = (f32[128]{0:T(128)S(1)}, f32[128]{0:T(128)S(1)}, u32[]{:S(2)}, u32[]{:S(2)}) collective-permute-start(f32[128]{0:T(128)S(1)} %add.90), channel_id=1, source_target_pairs={{0,1},{1,2},{2,3},{3,0},{4,5},{5,6},{6,7},{7,4},{8,9},{9,10},{10,1... | collective-permute-start | bytes 1544 | tf_op jit(solution)/shard_map/ppermute | solution.py:18
  239.0 5.4 %collective-permute-start.22 = (f32[128]{0:T(128)S(1)}, f32[128]{0:T(128)S(1)}, u32[]{:S(2)}, u32[]{:S(2)}) collective-permute-start(f32[128]{0:T(128)S(1)} %add.90), channel_id=1, source_target_pairs={{0,2},{1,3},{2,0},{3,1},{4,6},{5,7},{6,4},{7,5},{8,10},{9,11},{10,... | collective-permute-start | bytes 1544 | tf_op jit(solution)/shard_map/ppermute | solution.py:18
  240.2 2.1 collective-permute-start.25
